TPU v7x, 512 devices: a whole 4x8x8 slice. The times are simulated.
512 devices in a mesh: rows: 128 (over y, z, core), heads: 4 (over x).
Axes of the slice: x: 4, y: 8, z: 8, core: 2. Of those that a mesh axis runs over, the one named last changes fastest.
Arguments:
- imagery: bfloat16 [5, 8192, 1024], P(None, 'rows'), may hold values from -120 to 120
- stem_weight: bfloat16 [11520, 1024], P('rows', 'heads'), may hold values from -0.0546875 to 0.0546875
- token_gain: bfloat16 [1024], replicated, may hold values from 0.099609375 to 1.8984375
- latents: bfloat16 [512, 1024], replicated, may hold values from -6 to 6
- latent_gain: bfloat16 [1024], replicated, may hold values from 0.099609375 to 1.8984375
- query_weight: bfloat16 [1024, 1024], P('rows', 'heads'), may hold values from -1.5 to 1.5
- key_weight: bfloat16 [1024, 1024], P('rows', 'heads'), may hold values from -1.5 to 1.5
- value_weight: bfloat16 [1024, 1024], P('rows', 'heads'), may hold values from -0.1875 to 0.1875
- out_weight: bfloat16 [1024, 1024], P('rows', 'heads'), may hold values from -0.1875 to 0.1875
Outputs:
- latent_out: bfloat16 [512, 1024], P('rows', 'heads')
All inputs are finite; a program needn't handle non-finite values.
Results may differ from a plain program's by a relative error of at most 0.035.
The roundings to bfloat16 on the way count: a program that leaves them out, or rounds other values in their place, can miss the bound.
Values may be sent and summed in bfloat16 or wider, within the bound.
No kernel may reach another device: no remote copies, remote signals or barrier semaphores. Data moves between devices by JAX's collectives and lax.ppermute only.
A program may use at most 192 MiB of HBM per device.

v0:
```python
import jax
import jax.numpy as jnp
from jax import lax
from jax.sharding import PartitionSpec as P

D = 1024
HEADS = 16
LAT = 512
BANDS = 5
KER = 48
STRIDE = 32
TROWS = 2
TCOLS = 32


epsilon = 1e-05


def shifted(block, axis, distance):
    devices = range(lax.axis_size(axis))
    route = [(i - distance, i) for i in devices if i - distance in devices]
    return lax.ppermute(block, axis, route)


def layer_norm(inputs, gain_row):
    widened = inputs.astype(jnp.float32)
    average = jnp.mean(widened, axis=-1, keepdims=True)
    centered = widened - average
    variance = jnp.mean(centered * centered, axis=-1, keepdims=True)
    return (centered * lax.rsqrt(variance + epsilon) * gain_row.astype(jnp.float32)).astype(
        jnp.bfloat16
    )


def build_patches(strip_rows):
    rim_rows = KER - STRIDE
    padded = jnp.pad(strip_rows, ((0, 0), (0, STRIDE - rim_rows), (0, STRIDE)))
    blocks = padded.reshape(BANDS, TROWS + 1, STRIDE, TCOLS + 1, STRIDE)
    row_cat = jnp.concatenate([blocks[:, :TROWS], blocks[:, 1:, :rim_rows]], axis=2)
    col_cat = jnp.concatenate(
        [row_cat[:, :, :, :TCOLS, :], row_cat[:, :, :, 1:, :rim_rows]], axis=4
    )
    ordered = jnp.transpose(col_cat, (1, 3, 0, 2, 4))
    return ordered.reshape(TROWS * TCOLS, BANDS * KER * KER)


def per_device(
    imagery,
    stem_weight,
    token_gain,
    latents,
    latent_gain,
    query_weight,
    key_weight,
    value_weight,
    out_weight,
):
    rim_rows = KER - STRIDE
    below = shifted(imagery[:, :rim_rows, :], "rows", -1)
    patches = build_patches(jnp.concatenate([imagery, below], axis=1))
    token_count = patches.shape[0]
    width_dev = stem_weight.shape[1]
    stem_out = jnp.dot(
        patches,
        lax.all_gather(stem_weight, "rows", axis=0, tiled=True),
        preferred_element_type=jnp.float32,
    )
    feature = lax.all_gather(stem_out.astype(jnp.bfloat16), "heads", axis=1, tiled=True)
    token_norm = layer_norm(feature, token_gain)
    w_query, w_key, w_value, w_out = (
        lax.all_gather(query_weight, "rows", axis=0, tiled=True),
        lax.all_gather(key_weight, "rows", axis=0, tiled=True),
        lax.all_gather(value_weight, "rows", axis=0, tiled=True),
        lax.all_gather(out_weight, "rows", axis=0, tiled=True),
    )
    keys = jnp.dot(token_norm, w_key, preferred_element_type=jnp.float32).astype(jnp.bfloat16)
    values = jnp.dot(token_norm, w_value, preferred_element_type=jnp.float32).astype(jnp.bfloat16)
    head_size = D // HEADS
    heads_dev = width_dev // head_size
    latent_dev = LAT // lax.axis_size("rows")
    first_latent = lax.axis_index("rows") * latent_dev
    queries = jnp.dot(
        layer_norm(latents, latent_gain), w_query, preferred_element_type=jnp.float32
    ).astype(jnp.bfloat16)
    query_split = queries.reshape(LAT, heads_dev, head_size)
    key_split = keys.reshape(token_count, heads_dev, head_size)
    value_split = values.reshape(token_count, heads_dev, head_size)
    scores = jnp.einsum(
        "lhd,thd->lht", query_split, key_split, preferred_element_type=jnp.float32
    ) * head_size ** (-0.5)
    local_peak = jnp.max(scores, axis=2)

    def own_slice(array):
        return lax.dynamic_slice_in_dim(array, first_latent, latent_dev, 0)

    global_peak = lax.pmax(local_peak, "rows")
    weights = jnp.exp(scores - global_peak[:, :, None])
    totals = jnp.sum(weights, axis=2)
    upper_part = weights.astype(jnp.bfloat16)
    lower_part = (weights - upper_part.astype(jnp.float32)).astype(jnp.bfloat16)
    numerator = jnp.einsum(
        "lht,thd->lhd", upper_part, value_split, preferred_element_type=jnp.float32
    )
    numerator = numerator + jnp.einsum(
        "lht,thd->lhd", lower_part, value_split, preferred_element_type=jnp.float32
    )
    totals, numerator = (totals, numerator.reshape(LAT, width_dev))
    totals, numerator = lax.psum((totals, numerator), "rows")
    totals = own_slice(totals)
    numerator = own_slice(numerator)
    attended = numerator.reshape(latent_dev, heads_dev, head_size) / totals[:, :, None]
    mixed = attended.reshape(latent_dev, width_dev).astype(jnp.bfloat16)
    out_terms = lax.dot_general(
        mixed, w_out, (((1,), (1,)), ((), ())), preferred_element_type=jnp.float32
    )
    return lax.psum_scatter(out_terms, "heads", scatter_dimension=1, tiled=True).astype(
        jnp.bfloat16
    )


def solution(mesh):
    return jax.shard_map(
        per_device,
        mesh=mesh,
        in_specs=(
            P(None, "rows", None),
            P("rows", "heads"),
            P(),
            P(),
            P(),
            P("rows", "heads"),
            P("rows", "heads"),
            P("rows", "heads"),
            P("rows", "heads"),
        ),
        out_specs=P("rows", "heads"),
        check_vma=False,
    )
```

profile of v0, /device:TPU:1, one launch (start us, length us, event | category | flops | bytes accessed | tf_op | source)
XLA Modules:
  0.0 802.3 jit_solution(16675567579690148217)
XLA Ops:
  6.5 0.7 all-gather.3.cloned.1.call-update
  7.3 0.0 all-reduce.3.cloned.1.call-start
  7.3 0.9 slice.15
  8.2 8.8 %collective-permute-start = (bf16[5,16,1024]{2,1,0:T(8,128)(2,1)S(1)}, bf16[5,16,1024]{2,1,0:T(8,128)(2,1)S(1)}, u32[]{:S(2)}, u32[]{:S(2)}) collective-permute-start(bf16[5,16,1024]{2,1,0:T(8,128)(2,1)S(1)} %slice.15), channel_id=1, source_target_pairs={{4,0},{8,4},{12,8},{16,12},{20,16},{24,20},{28,24},{32,28},{36,32}... | collective-permute-start | bytes 491528 | tf_op jit(solution)/shard_map/ppermute | solution.py:22
  17.0 0.7 convert_element_type.54
  17.7 54.2 %all_gather.22 = bf16[1024,256]{1,0:T(8,128)(2,1)S(1)} all-gather(bf16[8,256]{1,0:T(8,128)(2,1)} %param.14), channel_id=1, replica_groups=mesh['rows'=128,'heads'=4] {'rows'}, dimensions={0}, use_global_device_ids=true | all-gather | bytes 528384 | tf_op jit(solution)/shard_map/all_gather | solution.py:71
  71.9 1.4 convert_reduce_fusion
  73.4 0.0 copy-start.5
  73.4 0.0 copy-start.3
  73.4 0.4 fusion.8
  73.9 0.7 convolution_convert_fusion
  74.6 48.4 %all_gather.21 = bf16[1024,256]{1,0:T(8,128)(2,1)S(1)} all-gather(bf16[8,256]{1,0:T(8,128)(2,1)S(1)} %copy-done.2), channel_id=1, replica_groups=mesh['rows'=128,'heads'=4] {'rows'}, dimensions={0}, use_global_device_ids=true | all-gather | bytes 528384 | tf_op jit(solution)/shard_map/all_gather | solution.py:72
  122.9 49.1 %all_gather.20 = bf16[1024,256]{1,0:T(8,128)(2,1)S(1)} all-gather(bf16[8,256]{1,0:T(8,128)(2,1)S(1)} %copy-done.3), channel_id=1, replica_groups=mesh['rows'=128,'heads'=4] {'rows'}, dimensions={0}, use_global_device_ids=true | all-gather | bytes 528384 | tf_op jit(solution)/shard_map/all_gather | solution.py:73
  172.1 0.0 collective-permute-done
  172.1 0.1 fusion.14
  172.2 4.6 reshape.49
  176.8 2.5 slice.20
  179.3 1.7 slice.21
  181.0 0.8 fusion
  181.8 3.5 fusion.2
  185.3 3.5 copy.17
  188.8 5.4 reshape.50
  194.2 0.0 all-gather.3.cloned.1.call-done
  194.2 9.4 %reshape.56 = bf16[11520,256]{1,0:T(8,128)(2,1)} reshape(bf16[128,90,256]{2,1,0:T(8,128)(2,1)} %all-gather.3.cloned.1.call-done) | data formatting | bytes 11796480
  203.6 3.8 convolution_convert_fusion.3
  207.4 9.7 %all_gather.19 = bf16[64,1024]{1,0:T(8,128)(2,1)S(1)} all-gather(bf16[64,256]{1,0:T(8,128)(2,1)S(1)} %convolution_convert_fusion.3), channel_id=1, replica_groups=mesh['rows'=128,'heads'=4] {'heads'}, dimensions={1}, use_global_device_ids=true | all-gather | bytes 163840 | tf_op jit(solution)/shard_map/all_gather | solution.py:68
  217.1 0.1 convert_reduce_fusion.1
  217.2 0.2 fusion.25
  217.4 0.3 convolution_convert_fusion.1
  217.7 0.1 reshape.52
  217.8 0.2 fusion.34
  218.0 0.0 copy-start.4
  218.0 253.0 %pmax.7 = f32[512,4]{0,1:T(4,128)S(1)} all-reduce(f32[512,4]{0,1:T(4,128)S(1)} %get-tuple-element.5), channel_id=1, replica_groups=mesh['rows'=128,'heads'=4] {'rows'}, use_global_device_ids=true, to_apply=%region_5.6 | all-reduce | flops 2048 | bytes 16384 | tf_op jit(solution)/shard_map/pmax | solution.py:96
  471.1 0.2 convolution_convert_fusion.2
  471.3 0.1 copy.23
  471.5 0.2 fusion.21
  471.7 1.0 convolution_add_fusion
  472.7 0.0 all-reduce.3.cloned.1.call-update
  472.8 0.0 reduce-scatter.4.cloned.1.call-start
  472.8 47.0 %all_gather.23 = bf16[1024,256]{1,0:T(8,128)(2,1)S(1)} all-gather(bf16[8,256]{1,0:T(8,128)(2,1)S(1)} %copy-done.4), channel_id=1, replica_groups=mesh['rows'=128,'heads'=4] {'rows'}, dimensions={0}, use_global_device_ids=true | all-gather | bytes 528384 | tf_op jit(solution)/shard_map/all_gather | solution.py:74
  519.9 0.1 fusion.19
  520.0 250.6 %psum.15 = f32[512,4]{0,1:T(4,128)S(1)} all-reduce(f32[512,4]{0,1:T(4,128)S(1)} %fusion.19), channel_id=1, replica_groups=mesh['rows'=128,'heads'=4] {'rows'}, use_global_device_ids=true, to_apply=%region_8.9 | all-reduce | flops 2048 | bytes 16384 | tf_op jit(solution)/shard_map/psum | solution.py:108
  770.6 0.1 constant_dynamic-slice_fusion
  770.6 1.0 fusion.30
  771.6 1.1 convolution_bitcast_fusion
  772.7 0.0 reduce-scatter.4.cloned.1.call-update
  772.8 21.5 %reduce-scatter.4.cloned.1.call-done = f32[256,4]{1,0:T(8,128)} async-done(((f32[1024,4]{1,0:T(8,128)}), f32[256,4]{1,0:T(8,128)}) %reduce-scatter.4.cloned.1.call-update) | async-done | bytes 4112
  794.2 1.6 copy.22
  (16 shorter events, 0.0 us)
Async XLA Ops:
  6.5 66.9 %copy-start = (bf16[512,1024]{1,0:T(8,128)(2,1)S(1)}, bf16[512,1024]{1,0:T(8,128)(2,1)}, u32[]{:S(2)}) copy-start(bf16[512,1024]{1,0:T(8,128)(2,1)} %param.12) | copy-start | bytes 3145732
  6.5 187.7 %all-gather.3.cloned.1.call-start = ((), (), s32[]{:S(2)}) async-start(), calls=%async_computation.2 | async-start | bytes 6340608 | tf_op jit(solution)/shard_map/all_gather | solution.py:65
  7.3 763.4 %all-reduce.3.cloned.1.call-start = ((), (), s32[]{:S(2)}) async-start(), calls=%async_computation.1 | async-start | bytes 1048576 | tf_op jit(solution)/shard_map/psum | solution.py:108
  8.2 163.8 %collective-permute-start = (bf16[5,16,1024]{2,1,0:T(8,128)(2,1)S(1)}, bf16[5,16,1024]{2,1,0:T(8,128)(2,1)S(1)}, u32[]{:S(2)}, u32[]{:S(2)}) collective-permute-start(bf16[5,16,1024]{2,1,0:T(8,128)(2,1)S(1)} %slice.15), channel_id=1, source_target_pairs={{4,0},{8,4},{12,8},{16,12},{20,16},{24,20},{28,24},{32,28},{36,32}... | collective-permute-start | bytes 491528 | tf_op jit(solution)/shard_map/ppermute | solution.py:22
  73.4 1.2 copy-start.2
  73.4 49.5 %copy-start.5 = (bf16[1024]{0:T(1024)(128)(2,1)S(1)}, bf16[1024]{0:T(1024)(128)(2,1)}, u32[]{:S(2)}) copy-start(bf16[1024]{0:T(1024)(128)(2,1)} %param.11) | copy-start | bytes 6148
  73.4 49.5 %copy-start.3 = (bf16[8,256]{1,0:T(8,128)(2,1)S(1)}, bf16[8,256]{1,0:T(8,128)(2,1)}, u32[]{:S(2)}) copy-start(bf16[8,256]{1,0:T(8,128)(2,1)} %param.16) | copy-start | bytes 12292
  73.8 98.3 %copy-start.1 = (bf16[5,64,1024]{2,1,0:T(8,128)(2,1)S(1)}, bf16[5,64,1024]{2,1,0:T(8,128)(2,1)}, u32[]{:S(2)}) copy-start(bf16[5,64,1024]{2,1,0:T(8,128)(2,1)} %param.9) | copy-start | bytes 1966084
  218.0 254.8 %copy-start.4 = (bf16[8,256]{1,0:T(8,128)(2,1)S(1)}, bf16[8,256]{1,0:T(8,128)(2,1)}, u32[]{:S(2)}) copy-start(bf16[8,256]{1,0:T(8,128)(2,1)} %param.17) | copy-start | bytes 12292
  472.8 321.5 %reduce-scatter.4.cloned.1.call-start = ((), (), s32[]{:S(2)}) async-start(), calls=%async_computation.3 | async-start | bytes 655360
Sparse Core Ops, SparseCore 0:
  10.5 92.5 all-gather.2
  472.9 183.7 all-reduce.2
  772.9 21.3 reduce-scatter.3
where the time goes:
time: 804 us; the launch traced here: 802 us
  blocking collectives  712 us (89%)
  local copies, waits for them, and re-layouts  29.9 us (4%)
  waiting for transfers between devices  22.2 us (3%)
  between operations  13.3 us (2%)
  starting transfers between devices  8.87 us (1%)
  other arithmetic  8.39 us (1%)
    pmax x1, blocking collectives, per_device(): global_peak = lax.pmax(local_peak, 'rows')  253 us
    psum x1, blocking collectives, per_device(): totals, numerator = lax.psum((totals, numerator), 'rows')  251 us
    all_gather x1, blocking collectives, per_device(): lax.all_gather(query_weight, 'rows', axis=0, tiled=True)  54.2 us
    all_gather x1, blocking collectives, per_device(): lax.all_gather(value_weight, 'rows', axis=0, tiled=True)  49.1 us
    all_gather x1, blocking collectives, per_device(): lax.all_gather(key_weight, 'rows', axis=0, tiled=True)  48.4 us
    all_gather x1, blocking collectives, per_device(): lax.all_gather(out_weight, 'rows', axis=0, tiled=True)  47 us
    unnamed x4, waiting for transfers between devices  22.2 us
  transfers between devices with their start and end apart: 4, of which 1 were waited for; matrix products, arithmetic and copies ran while one was open for 3% of the time, Pallas kernels for 0%

commit v1 on v0

v1 whole, which is shorter than its diff:
```python
import jax
import jax.numpy as jnp
from jax import lax
from jax.sharding import Mesh, PartitionSpec as P

D = 1024
HEADS = 16
LAT = 512
BANDS = 5
KER = 48
STRIDE = 32
TROWS = 2
TCOLS = 32
HEAD = D // HEADS

epsilon = 1e-05

ROWS = ("y", "z", "core")
SLOT = 128
STEM_SLOT = 96


def layer_norm(inputs, gain_row):
    widened = inputs.astype(jnp.float32)
    average = jnp.mean(widened, axis=-1, keepdims=True)
    centered = widened - average
    variance = jnp.mean(centered * centered, axis=-1, keepdims=True)
    return (centered * lax.rsqrt(variance + epsilon) * gain_row.astype(jnp.float32)).astype(
        jnp.bfloat16
    )


def build_patches(strip_rows):
    rim_rows = KER - STRIDE
    padded = jnp.pad(strip_rows, ((0, 0), (0, STRIDE - rim_rows), (0, STRIDE)))
    blocks = padded.reshape(BANDS, TROWS + 1, STRIDE, TCOLS + 1, STRIDE)
    row_cat = jnp.concatenate([blocks[:, :TROWS], blocks[:, 1:, :rim_rows]], axis=2)
    col_cat = jnp.concatenate(
        [row_cat[:, :, :, :TCOLS, :], row_cat[:, :, :, 1:, :rim_rows]], axis=4
    )
    ordered = jnp.transpose(col_cat, (1, 3, 0, 2, 4))
    return ordered.reshape(TROWS * TCOLS, BANDS * KER * KER)


def pieces(value):
    high = lax.reduce_precision(value, 8, 7)
    rest = value - high
    middle = lax.reduce_precision(rest, 8, 7)
    return [part.astype(jnp.bfloat16) for part in (high, middle, rest - middle)]


def per_device(
    imagery,
    stem_weight,
    token_gain,
    latents,
    latent_gain,
    query_weight,
    key_weight,
    value_weight,
    out_weight,
):
    rows = lax.axis_size(ROWS)
    rim_rows = KER - STRIDE
    own = stem_weight.shape[0]
    width = stem_weight.shape[1]
    heads_dev = width // HEAD
    latent_dev = LAT // rows

    packed = jnp.concatenate(
        [
            stem_weight,
            jnp.zeros((STEM_SLOT - own, width), jnp.bfloat16),
            query_weight,
            key_weight,
            value_weight,
            out_weight,
        ]
    )
    gathered = lax.all_gather(packed, ROWS, axis=0, tiled=True)

    below = lax.ppermute(imagery[:, :rim_rows, :], ROWS, [(i + 1, i) for i in range(rows - 1)])
    patches = build_patches(jnp.concatenate([imagery, below], axis=1))
    tokens = patches.shape[0]
    patches = jnp.pad(
        patches.reshape(tokens, rows, own), ((0, 0), (0, 0), (0, SLOT - own))
    ).reshape(tokens, rows * SLOT)
    latent_norm = layer_norm(latents, latent_gain)

    feature = jnp.dot(patches, gathered, preferred_element_type=jnp.float32).astype(jnp.bfloat16)
    feature = lax.all_to_all(
        jnp.broadcast_to(feature[None], (4,) + feature.shape), "heads", 0, 0
    )
    feature = jnp.transpose(feature, (1, 0, 2)).reshape(tokens, D)
    token_norm = layer_norm(feature, token_gain)

    slots = gathered.reshape(rows, SLOT, width)

    def projection(index):
        start = STEM_SLOT + 8 * index
        return slots[:, start : start + 8].reshape(D, width)

    queries = jnp.dot(latent_norm, projection(0), preferred_element_type=jnp.float32)
    keys = jnp.dot(token_norm, projection(1), preferred_element_type=jnp.float32)
    values = jnp.dot(token_norm, projection(2), preferred_element_type=jnp.float32)
    query_split = queries.astype(jnp.bfloat16).reshape(LAT, heads_dev, HEAD)
    key_split = keys.astype(jnp.bfloat16).reshape(tokens, heads_dev, HEAD)
    value_split = values.astype(jnp.bfloat16).reshape(tokens, heads_dev, HEAD)
    scores = jnp.einsum(
        "lhd,thd->lht", query_split, key_split, preferred_element_type=jnp.float32
    ) * HEAD ** (-0.5)
    peak = jnp.max(scores, axis=2)
    weights = jnp.exp(scores - peak[:, :, None])
    totals = jnp.sum(weights, axis=2)
    numerator = jnp.einsum(
        "lht,thd->lhd",
        weights.astype(jnp.bfloat16),
        value_split,
        preferred_element_type=jnp.float32,
    ).astype(jnp.bfloat16)

    stats = jnp.stack(pieces(peak) + pieces(totals), axis=1)
    stats = stats.reshape(rows, latent_dev * 6 * heads_dev)
    stats = jnp.pad(stats, ((0, 0), (0, 8 * 128 - stats.shape[1]))).reshape(rows, 8, 128)
    parcel = jnp.concatenate([numerator.reshape(rows, 8, 128), stats], axis=1)
    parcel = lax.all_to_all(parcel, ROWS, 0, 0)

    part = parcel[:, :8].reshape(rows, latent_dev, heads_dev, HEAD).astype(jnp.float32)
    stats = parcel[:, 8:].reshape(rows, 8 * 128)[:, : latent_dev * 6 * heads_dev]
    stats = stats.astype(jnp.float32).reshape(rows, latent_dev, 2, 3, heads_dev)
    stats = stats[:, :, :, 0] + stats[:, :, :, 1] + stats[:, :, :, 2]
    peak, totals = stats[:, :, 0], stats[:, :, 1]
    scale = jnp.exp(peak - jnp.max(peak, axis=0, keepdims=True))
    totals = jnp.sum(scale * totals, axis=0)
    mixed = jnp.sum(scale[..., None] * part, axis=0) / totals[..., None]
    mixed = mixed.reshape(latent_dev, width).astype(jnp.bfloat16)
    out_terms = lax.dot_general(
        mixed, projection(3), (((1,), (1,)), ((), ())), preferred_element_type=jnp.float32
    )
    out_terms = jnp.transpose(out_terms.reshape(latent_dev, 4, width), (1, 0, 2))
    out_terms = lax.all_to_all(out_terms, "heads", 0, 0)
    return jnp.sum(out_terms, axis=0).astype(jnp.bfloat16)


def solution(mesh):
    split = Mesh(mesh.devices.reshape(8, 8, 2, 4), ("y", "z", "core", "heads"))
    spread = P(ROWS, "heads")
    return jax.shard_map(
        per_device,
        mesh=split,
        in_specs=(P(None, ROWS, None), spread, P(), P(), P(), spread, spread, spread, spread),
        out_specs=spread,
        check_vma=False,
    )
```

time: 804 us -> 179 us (0.22)
  blocking collectives: 712 us -> 6.57 us
  waiting for transfers between devices: 22.2 us -> 76.6 us
  starting transfers between devices: 8.87 us -> 23.4 us
    pmax x1 -> x0, blocking collectives: 253 us -> none  [per_device(): global_peak = lax.pmax(local_peak, 'rows')]
    psum x1 -> x0, blocking collectives: 251 us -> none  [per_device(): totals, numerator = lax.psum((totals, numerator), 'rows')]
    all_gather x5 -> x0, blocking collectives: 208 us -> none  [the longest x1 54.2 us: per_device(): lax.all_gather(query_weight, 'rows', axis=0, tiled=True)]
    all_gather x1, waiting for transfers between devices: 0.02 us -> 55.1 us  [per_device(): gathered = lax.all_gather(packed, ROWS, axis=0, tiled=True)]
    unnamed x4 -> x1, waiting for transfers between devices: 22.2 us -> 0.02 us
    all_to_all x0 -> x2, waiting for transfers between devices: none -> 21.5 us  [the longest x1 18.4 us: per_device(): parcel = lax.all_to_all(parcel, ROWS, 0, 0)]
    all_to_all x0 -> x2, starting transfers between devices: none -> 14.7 us  [the longest x1 10.7 us: per_device(): parcel = lax.all_to_all(parcel, ROWS, 0, 0)]
    unnamed x14 -> x6, local copies, waits for them, and re-layouts: 11 us -> 0.11 us
  transfers between devices with their start and end apart: 4 -> 4, of which waited for: 1 -> 3; matrix products, arithmetic and copies ran while one was open for 3% -> 19% of each run, Pallas kernels for 0% -> 0%
where the time goes in v1:
time: 179 us; the launch traced here: 177 us
  waiting for transfers between devices  76.6 us (43%)
  local copies, waits for them, and re-layouts  36.7 us (21%)
  starting transfers between devices  23.4 us (13%)
  between operations  13.7 us (8%)
  matrix products  10.4 us (6%)
  other arithmetic  9.51 us (5%)
  blocking collectives  6.57 us (4%)
    all_gather x1, waiting for transfers between devices, per_device(): gathered = lax.all_gather(packed, ROWS, axis=0, tiled=True)  55.1 us
    all_to_all x1, waiting for transfers between devices, per_device(): parcel = lax.all_to_all(parcel, ROWS, 0, 0)  18.4 us
    all_to_all x1, starting transfers between devices, per_device(): parcel = lax.all_to_all(parcel, ROWS, 0, 0)  10.7 us
    ppermute x1, starting transfers between devices, per_device(): lax.ppermute(imagery[:, :rim_rows, :], ROWS, [(i + 1, i) for i in range(r...  8.79 us
    concatenate x1, local copies, waits for them, and re-layouts, per_device(): jnp.concatenate([stem_weight, jnp.zeros((STEM_SLOT - own, width), jnp.bfl...  7.94 us
    another operation x1, local copies, waits for them, and re-layouts, per_device(): patches.reshape(tokens, rows, own)  7.15 us
    all_to_all x1, blocking collectives, per_device(): out_terms = lax.all_to_all(out_terms, 'heads', 0, 0)  6.57 us
    dot_general x1, matrix products, per_device(): jnp.dot(patches, gathered, preferred_element_type=jnp.float32)  5.52 us
  transfers between devices with their start and end apart: 4, of which 3 were waited for; matrix products, arithmetic and copies ran while one was open for 19% of the time, Pallas kernels for 0%

profile of v1, /device:TPU:1, one launch (start us, length us, event | category | flops | bytes accessed | tf_op | source)
XLA Modules:
  0.0 177.0 jit_solution(5652178805205751695)
XLA Ops:
  6.5 7.9 %concatenate.18 = bf16[128,256]{1,0:T(8,128)(2,1)} concatenate(bf16[90,256]{1,0:T(8,128)(2,1)} %param.10, bf16[6,256]{1,0:T(8,128)(2,1)S(1)} %broadcast_in_dim.4, bf16[8,256]{1,0:T(8,128)(2,1)} %param.14, bf16[8,256]{1,0:T(8,128)(2,1)} %param.15, bf16[8,256]{1,0:T(8,128)(2,1)} %param.16, bf16[8,256]{1,0:T(8,128)(2,1)} %param.17), dimensions={0} | concatenate | bytes 131072 | tf_op jit(solution)/shard_map/concatenate | solution.py:70
  14.5 0.9 slice.51
  15.4 8.8 %collective-permute-start = (bf16[5,16,1024]{2,1,0:T(8,128)(2,1)S(1)}, bf16[5,16,1024]{2,1,0:T(8,128)(2,1)S(1)}, u32[]{:S(2)}, u32[]{:S(2)}) collective-permute-start(bf16[5,16,1024]{2,1,0:T(8,128)(2,1)S(1)} %slice.51), channel_id=1, source_target_pairs={{4,0},{8,4},{12,8},{16,12},{20,16},{24,20},{28,24},{32,28},{36,32}... | collective-permute-start | bytes 491528 | tf_op jit(solution)/shard_map/ppermute | solution.py:82
  24.2 0.7 reshape.225
  24.9 0.7 convert_element_type.136
  25.6 1.4 convert_reduce_fusion
  27.1 0.4 fusion.8
  27.5 0.1 fusion.21
  27.6 4.6 %reshape.210 = bf16[5,3,32,33,32]{4,3,2,1,0:T(8,128)(2,1)} reshape(bf16[5,96,1056]{2,1,0:T(8,128)(2,1)S(1)} %fusion.21) | data formatting | bytes 2027520 | tf_op jit(solution)/shard_map/reshape | solution.py:36
  32.2 2.5 %slice.68 = bf16[5,2,32,33,32]{4,3,2,1,0:T(8,128)(2,1)S(1)} slice(bf16[5,3,32,33,32]{4,3,2,1,0:T(8,128)(2,1)} %reshape.210), slice={[0:5], [0:2], [0:32], [0:33], [0:32]} | slice | bytes 1351680 | tf_op jit(solution)/shard_map/slice | solution.py:37
  34.7 1.7 slice.69
  36.5 0.8 fusion
  37.3 3.5 %fusion.2 = bf16[2,32,5,48,48]{4,1,3,0,2:T(8,128)(2,1)S(1)} fusion(bf16[5,2,16,33,32]{4,3,2,1,0:T(8,128)(2,1)S(1)} %slice.69, bf16[5,2,32,33,32]{4,3,2,1,0:T(8,128)(2,1)S(1)} %slice.68, bf16[5,2,48,32,32]{4,3,2,1,0:T(8,128)(2,1)S(1)} %fusion), kind=kLoop, calls=%fused_computation.5 | loop fusion | flops 4423680 | bytes 3471360 | tf_op jit(solution)/shard_map/transpose | solution.py:41
  40.8 3.4 %copy.23 = bf16[2,32,5,48,48]{4,3,2,1,0:T(8,128)(2,1)} copy(bf16[2,32,5,48,48]{4,1,3,0,2:T(8,128)(2,1)S(1)} %fusion.2) | data formatting | bytes 2949120 | tf_op jit(solution)/shard_map/transpose | solution.py:41
  44.2 7.2 %reshape_reshape.3 = bf16[64,128,90]{2,1,0:T(8,128)(2,1)} reshape(bf16[2,32,5,48,48]{4,3,2,1,0:T(8,128)(2,1)} %copy.23) | data formatting | bytes 2949120 | tf_op jit(solution)/shard_map/reshape;reshape | solution.py:86
  51.4 2.2 %pad.13 = bf16[64,128,128]{2,1,0:T(8,128)(2,1)S(1)} pad(bf16[64,128,90]{2,1,0:T(8,128)(2,1)} %reshape_reshape.3, bf16[]{:T(256)} %constant.6.clone.1), padding=0_0x0_0x0_38 | pad | bytes 3571714 | tf_op jit(solution)/shard_map/jit(_pad)/pad | solution.py:85
  53.5 55.1 %all-gather.2.cloned.1.call-done = bf16[16384,256]{1,0:T(8,128)(2,1)} async-done(((bf16[128,256]{1,0:T(8,128)(2,1)}), bf16[16384,256]{1,0:T(8,128)(2,1)}) %all-gather.2.cloned.1.call-update) | async-done | bytes 8388624 | tf_op jit(solution)/shard_map/all_gather | solution.py:80
  108.7 5.5 %fusion.18 = bf16[64,256]{1,0:T(8,128)(2,1)S(1)} fusion(bf16[16384,256]{1,0:T(8,128)(2,1)} %all-gather.2.cloned.1.call-done, bf16[8,8,128,128]{3,2,1,0:T(8,128)(2,1)S(1)} %bitcast.93), kind=kOutput, calls=%fused_computation.28 | convolution fusion | flops 536887296 | bytes 10518528 | tf_op jit(solution)/shard_map/dot_general | solution.py:90
  114.2 0.7 broadcast_in_dim.5
  114.9 4.0 %all-to-all-start = ((bf16[4,64,256]{2,1,0:T(8,128)(2,1)}), bf16[4,64,256]{2,1,0:T(8,128)(2,1)S(1)}, u32[]{:S(2)}, u32[]{:S(2)}) async-start(bf16[4,64,256]{2,1,0:T(8,128)(2,1)} %broadcast_in_dim.5), calls=%async_computation | async-start | bytes 262144 | tf_op jit(solution)/shard_map/all_to_all | solution.py:91
  118.9 1.7 convolution_convert_fusion.1
  120.6 3.1 %all-to-all-done = bf16[4,64,256]{2,1,0:T(8,128)(2,1)S(1)} async-done(((bf16[4,64,256]{2,1,0:T(8,128)(2,1)}), bf16[4,64,256]{2,1,0:T(8,128)(2,1)S(1)}, u32[]{:S(2)}, u32[]{:S(2)}) %all-to-all-start) | async-done | bytes 131104 | tf_op jit(solution)/shard_map/all_to_all | solution.py:91
  123.7 0.1 convert_reduce_fusion.1
  123.8 0.2 fusion.30
  124.0 0.1 fusion.35
  124.2 1.2 convolution_convert_fusion.2
  125.4 1.2 convolution_convert_fusion.3
  126.7 0.1 reshape.216
  126.8 0.1 copy.32
  126.9 0.2 fusion.44
  127.1 0.1 fusion.26
  127.2 0.2 fusion.17
  127.5 0.3 copy.27
  127.8 0.2 reshape.219
  128.1 0.7 copy.28
  128.8 1.5 reshape.220
  130.5 0.9 pad_maximum_fusion.1
  131.4 10.7 %all-to-all-start.1 = ((bf16[128,16,128]{2,1,0:T(8,128)(2,1)}), bf16[128,16,128]{2,1,0:T(8,128)(2,1)S(1)}, u32[]{:S(2)}, u32[]{:S(2)}) async-start(bf16[128,16,128]{2,1,0:T(8,128)(2,1)} %pad_maximum_fusion.1), calls=%async_computation.1 | async-start | bytes 1048576 | tf_op jit(solution)/shard_map/all_to_all | solution.py:126
  142.1 1.1 slice.83
  143.2 18.4 %all-to-all-done.1 = bf16[128,16,128]{2,1,0:T(8,128)(2,1)S(1)} async-done(((bf16[128,16,128]{2,1,0:T(8,128)(2,1)}), bf16[128,16,128]{2,1,0:T(8,128)(2,1)S(1)}, u32[]{:S(2)}, u32[]{:S(2)}) %all-to-all-start.1) | async-done | bytes 524320 | tf_op jit(solution)/shard_map/all_to_all | solution.py:126
  161.6 0.2 copy.33
  161.9 0.1 bitcast_reduce_fusion
  162.0 0.2 fusion.41
  162.2 0.2 copy.31
  162.6 0.1 multiply_reduce_fusion
  162.7 0.2 convolution_bitcast_fusion
  163.0 6.6 %all_to_all.15 = f32[4,4,256]{2,1,0:T(4,128)S(1)} all-to-all(f32[4,4,256]{2,1,0:T(4,128)S(1)} %convolution_bitcast_fusion), channel_id=1, replica_groups=mesh['y'=8,'z'=8,'core'=2,'heads'=4] {'heads'}, dimensions={0} | all-to-all | bytes 32768 | tf_op jit(solution)/shard_map/all_to_all | solution.py:141
  169.5 0.6 reduce_sum.82
  (30 shorter events, 0.5 us)
Async XLA Ops:
  6.5 20.5 %copy-start = (bf16[512,1024]{1,0:T(8,128)(2,1)S(1)}, bf16[512,1024]{1,0:T(8,128)(2,1)}, u32[]{:S(2)}) copy-start(bf16[512,1024]{1,0:T(8,128)(2,1)} %param.12) | copy-start | bytes 3145732
  6.5 21.0 %copy-start.1 = (bf16[5,64,1024]{2,1,0:T(8,128)(2,1)S(1)}, bf16[5,64,1024]{2,1,0:T(8,128)(2,1)}, u32[]{:S(2)}) copy-start(bf16[5,64,1024]{2,1,0:T(8,128)(2,1)} %param.9) | copy-start | bytes 1966084
  6.5 102.2 %all-gather.2.cloned.1.call-start = ((), (), s32[]{:S(2)}) async-start(), calls=%async_computation.3 | async-start | bytes 8454144 | tf_op jit(solution)/shard_map/all_gather | solution.py:80
  15.4 12.0 %collective-permute-start = (bf16[5,16,1024]{2,1,0:T(8,128)(2,1)S(1)}, bf16[5,16,1024]{2,1,0:T(8,128)(2,1)S(1)}, u32[]{:S(2)}, u32[]{:S(2)}) collective-permute-start(bf16[5,16,1024]{2,1,0:T(8,128)(2,1)S(1)} %slice.51), channel_id=1, source_target_pairs={{4,0},{8,4},{12,8},{16,12},{20,16},{24,20},{28,24},{32,28},{36,32}... | collective-permute-start | bytes 491528 | tf_op jit(solution)/shard_map/ppermute | solution.py:82
  114.9 8.8 %all-to-all-start = ((bf16[4,64,256]{2,1,0:T(8,128)(2,1)}), bf16[4,64,256]{2,1,0:T(8,128)(2,1)S(1)}, u32[]{:S(2)}, u32[]{:S(2)}) async-start(bf16[4,64,256]{2,1,0:T(8,128)(2,1)} %broadcast_in_dim.5), calls=%async_computation | async-start | bytes 262144 | tf_op jit(solution)/shard_map/all_to_all | solution.py:91
  131.4 30.2 %all-to-all-start.1 = ((bf16[128,16,128]{2,1,0:T(8,128)(2,1)}), bf16[128,16,128]{2,1,0:T(8,128)(2,1)S(1)}, u32[]{:S(2)}, u32[]{:S(2)}) async-start(bf16[128,16,128]{2,1,0:T(8,128)(2,1)} %pad_maximum_fusion.1), calls=%async_computation.1 | async-start | bytes 1048576 | tf_op jit(solution)/shard_map/all_to_all | solution.py:126
Sparse Core Ops, SparseCore 0:
  14.6 94.0 all-gather.1

commit v2 on v1

v2 whole, which is shorter than its diff:
```python
import jax
import jax.numpy as jnp
from jax import lax
from jax.sharding import Mesh, PartitionSpec as P

D = 1024
HEADS = 16
LAT = 512
BANDS = 5
KER = 48
STRIDE = 32
TROWS = 4
TCOLS = 32
HEAD = D // HEADS

epsilon = 1e-05

ROWS = ("y", "z", "core")
CHIPS = ("y", "z")
SHARE = ("heads", "core")
SLOT = 128
STEM_AT = 32
HALF = 128


def layer_norm(inputs, gain_row):
    widened = inputs.astype(jnp.float32)
    average = jnp.mean(widened, axis=-1, keepdims=True)
    centered = widened - average
    variance = jnp.mean(centered * centered, axis=-1, keepdims=True)
    return (centered * lax.rsqrt(variance + epsilon) * gain_row.astype(jnp.float32)).astype(
        jnp.bfloat16
    )


def build_patches(strip_rows):
    rim_rows = KER - STRIDE
    padded = jnp.pad(strip_rows, ((0, 0), (0, STRIDE - rim_rows), (0, STRIDE)))
    blocks = padded.reshape(BANDS, TROWS + 1, STRIDE, TCOLS + 1, STRIDE)
    row_cat = jnp.concatenate([blocks[:, :TROWS], blocks[:, 1:, :rim_rows]], axis=2)
    col_cat = jnp.concatenate(
        [row_cat[:, :, :, :TCOLS, :], row_cat[:, :, :, 1:, :rim_rows]], axis=4
    )
    ordered = jnp.transpose(col_cat, (1, 3, 0, 2, 4))
    return ordered.reshape(TROWS * TCOLS, BANDS * KER * KER)


def pieces(value):
    high = lax.reduce_precision(value, 8, 7)
    rest = value - high
    middle = lax.reduce_precision(rest, 8, 7)
    return [part.astype(jnp.bfloat16) for part in (high, middle, rest - middle)]


def chip_image(imagery):
    rows = lax.axis_size(ROWS)
    rim = imagery[:, : KER - STRIDE]
    other = lax.ppermute(imagery, "core", [(0, 1), (1, 0)])
    below_even = lax.ppermute(rim, ROWS, [(r + 2, r) for r in range(0, rows - 2, 2)])
    below_odd = lax.ppermute(rim, ROWS, [(r + 1, r) for r in range(1, rows - 2, 2)])
    first = lax.axis_index("core") == 0
    upper = jnp.where(first, imagery, other)
    lower = jnp.where(first, other, imagery)
    below = jnp.where(first, below_even, below_odd)
    return jnp.concatenate([upper, lower, below], axis=1)


def per_device(
    imagery,
    stem_weight,
    token_gain,
    latents,
    latent_gain,
    query_weight,
    key_weight,
    value_weight,
    out_weight,
):
    rows = lax.axis_size(ROWS)
    chips = rows // 2
    own = stem_weight.shape[0]
    width = stem_weight.shape[1]
    heads_core = HALF // HEAD
    latent_chip = LAT // chips

    packed = jnp.concatenate(
        [
            query_weight,
            key_weight,
            value_weight,
            out_weight,
            jnp.pad(stem_weight, ((0, SLOT - STEM_AT - own), (0, 0))),
        ]
    )
    halves = jnp.stack([packed[:, :HALF], packed[:, HALF:]])
    spread = jnp.broadcast_to(halves[None], (8, 2, SLOT, HALF)).reshape(16, SLOT, HALF)
    plane = lax.all_to_all(spread, ("z", "core"), 0, 0)
    gathered = lax.all_gather(plane.reshape(16 * SLOT, HALF), "y", axis=0, tiled=True)

    patches = build_patches(chip_image(imagery))
    tokens = patches.shape[0]
    patches = jnp.pad(
        patches.reshape(tokens, rows, own),
        ((0, 0), (0, 0), (STEM_AT, SLOT - STEM_AT - own)),
    ).reshape(tokens, rows * SLOT)
    latent_norm = layer_norm(latents, latent_gain)

    feature = jnp.dot(patches, gathered, preferred_element_type=jnp.float32).astype(jnp.bfloat16)
    feature = lax.all_to_all(
        jnp.broadcast_to(feature[None], (8,) + feature.shape), SHARE, 0, 0
    )
    feature = jnp.transpose(feature, (1, 0, 2)).reshape(tokens, D)
    token_norm = layer_norm(feature, token_gain)

    slots = gathered.reshape(rows, SLOT, HALF)

    def projection(index):
        return slots[:, 8 * index : 8 * index + 8].reshape(D, HALF)

    queries = jnp.dot(latent_norm, projection(0), preferred_element_type=jnp.float32)
    keys = jnp.dot(token_norm, projection(1), preferred_element_type=jnp.float32)
    values = jnp.dot(token_norm, projection(2), preferred_element_type=jnp.float32)
    query_split = queries.astype(jnp.bfloat16).reshape(LAT, heads_core, HEAD)
    key_split = keys.astype(jnp.bfloat16).reshape(tokens, heads_core, HEAD)
    value_split = values.astype(jnp.bfloat16).reshape(tokens, heads_core, HEAD)
    scores = jnp.einsum(
        "lhd,thd->lht", query_split, key_split, preferred_element_type=jnp.float32
    ) * HEAD ** (-0.5)
    peak = jnp.max(scores, axis=2)
    weights = jnp.exp(scores - peak[:, :, None])
    totals = jnp.sum(weights, axis=2)
    numerator = jnp.einsum(
        "lht,thd->lhd",
        weights.astype(jnp.bfloat16),
        value_split,
        preferred_element_type=jnp.float32,
    ).astype(jnp.bfloat16)

    stats = jnp.stack(pieces(peak) + pieces(totals), axis=2)
    stats = jnp.pad(stats, ((0, 0), (0, 0), (0, HEAD - 6))).reshape(chips, latent_chip, HALF)
    parcel = jnp.concatenate([numerator.reshape(chips, latent_chip, HALF), stats], axis=1)
    parcel = lax.all_to_all(parcel, CHIPS, 0, 0)

    parcel = parcel.astype(jnp.float32).reshape(chips, 2, latent_chip, heads_core, HEAD)
    part, stats = parcel[:, 0], parcel[:, 1]
    peak = stats[..., 0:1] + stats[..., 1:2] + stats[..., 2:3]
    totals = stats[..., 3:4] + stats[..., 4:5] + stats[..., 5:6]
    scale = jnp.exp(peak - jnp.max(peak, axis=0, keepdims=True))
    totals = jnp.sum(scale * totals, axis=0)
    mixed = jnp.sum(scale * part, axis=0) / totals
    mixed = mixed.reshape(latent_chip, HALF).astype(jnp.bfloat16)
    out_terms = lax.dot_general(
        mixed, projection(3), (((1,), (1,)), ((), ())), preferred_element_type=jnp.float32
    )
    out_terms = out_terms.reshape(2, latent_chip // 2, D // width, width)
    out_terms = jnp.transpose(out_terms, (2, 0, 1, 3)).reshape(8, latent_chip // 2, width)
    out_terms = lax.all_to_all(out_terms, SHARE, 0, 0)
    return jnp.sum(out_terms, axis=0).astype(jnp.bfloat16)


def solution(mesh):
    split = Mesh(mesh.devices.reshape(8, 8, 2, 4), ("y", "z", "core", "heads"))
    spread = P(ROWS, "heads")
    return jax.shard_map(
        per_device,
        mesh=split,
        in_specs=(P(None, ROWS, None), spread, P(), P(), P(), spread, spread, spread, spread),
        out_specs=spread,
        check_vma=False,
    )
```

time: 179 us -> 170 us (0.950)
  waiting for transfers between devices: 76.6 us -> 16.3 us
  blocking collectives: 6.57 us -> 39.7 us
  local copies, waits for them, and re-layouts: 36.7 us -> 49.1 us
  other arithmetic: 9.51 us -> 17.9 us
  starting transfers between devices: 23.4 us -> 21.1 us
    all_gather x1, waiting for transfers between devices: 55.1 us -> 0.01 us  [per_device(): lax.all_gather(plane.reshape(16 * SLOT, HALF), 'y', axis=0, tiled=True)]
    all_to_all x1 -> x2, blocking collectives: 6.57 us -> 39.7 us  [the longest x1 29.1 us: per_device(): plane = lax.all_to_all(spread, ('z', 'core'), 0, 0)]
    concatenate x1, local copies, waits for them, and re-layouts: 7.94 us -> 0.8 us  [per_device(): jnp.concatenate([query_weight, key_weight, value_weight, out_weight, jnp....]
    another operation x1, local copies, waits for them, and re-layouts: 7.15 us -> 13.1 us  [per_device(): patches.reshape(tokens, rows, own)]
    all_to_all x2, waiting for transfers between devices: 21.5 us -> 16.1 us  [the longest x1 11.3 us: per_device(): parcel = lax.all_to_all(parcel, CHIPS, 0, 0)]
    ppermute x1 -> x3, starting transfers between devices: 8.79 us -> 3.89 us  [the longest x1 1.92 us: chip_image(): other = lax.ppermute(imagery, 'core', [(0, 1), (1, 0)])]
    pad x1 -> x2, local copies, waits for them, and re-layouts: 2.16 us -> 5.87 us  [the longest x1 5.59 us: per_device(): jnp.pad(patches.reshape(tokens, rows, own), ((0, 0), (0, 0), (STEM_AT, SL...]
    transpose x1, other arithmetic: 3.5 us -> 6.97 us  [build_patches(): ordered = jnp.transpose(col_cat, (1, 3, 0, 2, 4))]
  transfers between devices with their start and end apart: 4 -> 6, of which waited for: 3 -> 3; matrix products, arithmetic and copies ran while one was open for 19% -> 32% of each run, Pallas kernels for 0% -> 0%
where the time goes in v2:
time: 170 us; the launch traced here: 169 us
  local copies, waits for them, and re-layouts  49.1 us (29%)
  blocking collectives  39.7 us (23%)
  starting transfers between devices  21.1 us (12%)
  other arithmetic  17.9 us (11%)
  waiting for transfers between devices  16.3 us (10%)
  between operations  13.7 us (8%)
  matrix products  10.8 us (6%)
    all_to_all x1, blocking collectives, per_device(): plane = lax.all_to_all(spread, ('z', 'core'), 0, 0)  29.1 us
    another operation x1, local copies, waits for them, and re-layouts, per_device(): patches.reshape(tokens, rows, own)  13.1 us
    all_to_all x1, starting transfers between devices, per_device(): parcel = lax.all_to_all(parcel, CHIPS, 0, 0)  12.5 us
    all_to_all x1, waiting for transfers between devices, per_device(): parcel = lax.all_to_all(parcel, CHIPS, 0, 0)  11.3 us
    all_to_all x1, blocking collectives, per_device(): out_terms = lax.all_to_all(out_terms, SHARE, 0, 0)  10.6 us
    transpose x1, other arithmetic, build_patches(): ordered = jnp.transpose(col_cat, (1, 3, 0, 2, 4))  6.97 us
    reshape x1, local copies, waits for them, and re-layouts, build_patches(): blocks = padded.reshape(BANDS, TROWS + 1, STRIDE, TCOLS + 1, STRIDE)  6.45 us
    dot_general x1, matrix products, per_device(): jnp.dot(patches, gathered, preferred_element_type=jnp.float32)  6.11 us
  transfers between devices with their start and end apart: 6, of which 3 were waited for; matrix products, arithmetic and copies ran while one was open for 32% of the time, Pallas kernels for 0%

profile of v2, /device:TPU:1, one launch (start us, length us, event | category | flops | bytes accessed | tf_op | source)
XLA Modules:
  0.0 168.6 jit_solution(10345270459264976293)
XLA Ops:
  6.5 0.8 constant_dynamic-update-slice_fusion.3
  7.4 0.7 constant_dynamic-update-slice_fusion.2
  8.0 0.7 constant_dynamic-update-slice_fusion.1
  8.7 0.7 constant_dynamic-update-slice_fusion
  9.4 0.8 pad_dynamic-update-slice_fusion
  10.4 29.1 %all_to_all.20 = bf16[16,128,128]{2,1,0:T(8,128)(2,1)} all-to-all(bf16[16,128,128]{2,1,0:T(8,128)(2,1)S(1)} %bitcast.93), channel_id=1, replica_groups=mesh['y'=8,'z'=8,'core'=2,'heads'=4] {'z','core'}, dimensions={0} | all-to-all | bytes 1048576 | tf_op jit(solution)/shard_map/all_to_all | solution.py:97
  39.4 0.9 slice.57
  40.4 0.7 collective-permute-start.1
  41.0 1.3 collective-permute-start.2
  42.3 1.9 %collective-permute-start = (bf16[5,64,1024]{2,1,0:T(8,128)(2,1)}, bf16[5,64,1024]{2,1,0:T(8,128)(2,1)S(1)}, u32[]{:S(2)}, u32[]{:S(2)}) collective-permute-start(bf16[5,64,1024]{2,1,0:T(8,128)(2,1)} %param.9), channel_id=1, source_target_pairs={{0,4},{4,0},{1,5},{5,1},{2,6},{6,2},{3,7},{7,3},{8,12},{12,8},{9,1... | collective-permute-start | bytes 1966088 | tf_op jit(solution)/shard_map/ppermute | solution.py:58
  44.3 1.4 convert_reduce_fusion
  45.7 0.7 bitcast_convert_fusion
  46.4 0.7 convert_element_type.135
  47.1 0.4 fusion.15
  47.5 0.2 collective-permute-done.2
  48.0 6.5 %reshape.208 = bf16[5,5,32,33,32]{4,3,2,1,0:T(8,128)(2,1)} reshape(bf16[5,160,1056]{2,1,0:T(8,128)(2,1)S(1)} %fusion.19) | data formatting | bytes 3379200 | tf_op jit(solution)/shard_map/reshape | solution.py:39
  54.4 4.0 %slice.76 = bf16[5,4,32,33,32]{4,3,2,1,0:T(8,128)(2,1)S(1)} slice(bf16[5,5,32,33,32]{4,3,2,1,0:T(8,128)(2,1)} %reshape.208), slice={[0:5], [0:4], [0:32], [0:33], [0:32]} | slice | bytes 2703360 | tf_op jit(solution)/shard_map/slice | solution.py:40
  58.5 2.5 %slice.77 = bf16[5,4,16,33,32]{4,3,2,1,0:T(8,128)(2,1)S(1)} slice(bf16[5,5,32,33,32]{4,3,2,1,0:T(8,128)(2,1)} %reshape.208), slice={[0:5], [1:5], [0:16], [0:33], [0:32]} | slice | bytes 1351680 | tf_op jit(solution)/shard_map/slice | solution.py:40
  61.0 1.6 fusion
  62.6 7.0 %fusion.2 = bf16[4,32,5,48,48]{4,1,3,0,2:T(8,128)(2,1)S(1)} fusion(bf16[5,4,16,33,32]{4,3,2,1,0:T(8,128)(2,1)S(1)} %slice.77, bf16[5,4,32,33,32]{4,3,2,1,0:T(8,128)(2,1)S(1)} %slice.76, bf16[5,4,48,32,32]{4,3,2,1,0:T(8,128)(2,1)S(1)} %fusion), kind=kLoop, calls=%fused_computation.5 | loop fusion | flops 8847360 | bytes 6942720 | tf_op jit(solution)/shard_map/transpose | solution.py:44
  69.6 6.1 %copy.17 = bf16[4,32,5,48,48]{4,3,2,1,0:T(8,128)(2,1)} copy(bf16[4,32,5,48,48]{4,1,3,0,2:T(8,128)(2,1)S(1)} %fusion.2) | data formatting | bytes 5898240 | tf_op jit(solution)/shard_map/transpose | solution.py:44
  75.7 13.1 %reshape_reshape.3 = bf16[128,128,90]{2,1,0:T(8,128)(2,1)} reshape(bf16[4,32,5,48,48]{4,3,2,1,0:T(8,128)(2,1)} %copy.17) | data formatting | bytes 5898240 | tf_op jit(solution)/shard_map/reshape;reshape | solution.py:103
  88.8 5.6 %pad.17 = bf16[128,128,128]{2,1,0:T(8,128)(2,1)} pad(bf16[128,128,90]{2,1,0:T(8,128)(2,1)} %reshape_reshape.3, bf16[]{:T(256)} %constant.20.clone.1), padding=0_0x0_0x32_6 | pad | bytes 7143426 | tf_op jit(solution)/shard_map/jit(_pad)/pad | solution.py:102
  94.4 6.1 %fusion.22 = bf16[128,128]{1,0:T(8,128)(2,1)S(1)} fusion(bf16[16384,128]{1,0:T(8,128)(2,1)} %all-gather.2.cloned.1.call-done, bf16[16,8,128,128]{3,2,1,0:T(8,128)(2,1)} %bitcast.91), kind=kOutput, calls=%fused_computation.32 | convolution fusion | flops 536887296 | bytes 8421376 | tf_op jit(solution)/shard_map/dot_general | solution.py:108
  100.6 0.7 broadcast_in_dim.5
  101.3 4.7 %all-to-all-start.1 = ((bf16[8,128,128]{1,2,0:T(8,128)(2,1)}), bf16[8,128,128]{1,2,0:T(8,128)(2,1)S(1)}, u32[]{:S(2)}, u32[]{:S(2)}) async-start(bf16[8,128,128]{1,2,0:T(8,128)(2,1)} %broadcast_in_dim.5), calls=%async_computation.1 | async-start | bytes 524288 | tf_op jit(solution)/shard_map/all_to_all | solution.py:109
  106.0 1.6 convolution_convert_fusion.1
  107.6 4.9 %all-to-all-done.1 = bf16[8,128,128]{1,2,0:T(8,128)(2,1)S(1)} async-done(((bf16[8,128,128]{1,2,0:T(8,128)(2,1)}), bf16[8,128,128]{1,2,0:T(8,128)(2,1)S(1)}, u32[]{:S(2)}, u32[]{:S(2)}) %all-to-all-start.1) | async-done | bytes 262176 | tf_op jit(solution)/shard_map/all_to_all | solution.py:109
  112.8 0.2 fusion.33
  113.0 1.2 convolution_convert_fusion.3
  114.3 1.2 convolution_convert_fusion.2
  115.5 0.3 fusion.46
  115.9 0.2 fusion.21
  116.1 0.2 copy.20
  116.5 0.2 copy.28
  116.8 0.3 pad.19.clone
  117.2 0.7 pad_maximum_fusion.1
  117.9 12.5 %all-to-all-start.2 = ((bf16[64,16,128]{2,1,0:T(8,128)(2,1)}), bf16[64,16,128]{2,1,0:T(8,128)(2,1)S(1)}, u32[]{:S(2)}, u32[]{:S(2)}) async-start(bf16[64,16,128]{2,1,0:T(8,128)(2,1)} %pad_maximum_fusion.1), calls=%async_computation.2 | async-start | bytes 524288 | tf_op jit(solution)/shard_map/all_to_all | solution.py:142
  130.5 1.0 slice.93
  131.5 11.3 %all-to-all-done.2 = bf16[64,16,128]{2,1,0:T(8,128)(2,1)S(1)} async-done(((bf16[64,16,128]{2,1,0:T(8,128)(2,1)}), bf16[64,16,128]{2,1,0:T(8,128)(2,1)S(1)}, u32[]{:S(2)}, u32[]{:S(2)}) %all-to-all-start.2) | async-done | bytes 262176 | tf_op jit(solution)/shard_map/all_to_all | solution.py:142
  142.7 0.6 reshape.226
  143.4 1.2 fusion.45
  144.6 1.8 %fusion.37 = (f32[8,2]{1,0:T(8,128)S(1)}, f32[64,8,2,1]{3,2,1,0:T(2,128)S(1)}) fusion(f32[64,8,2,64]{3,2,1,0:T(2,128)S(1)} %slice_bitcast_fusion.1, f32[64,8,2,1]{3,2,1,0:T(2,128)S(1)} %get-tuple-element.8, f32[8,2]{1,0:T(8,128)S(1)} %get-tuple-element.7), kind=kLoop, calls=%fused_computation.59 | loop fusion | flops 5104 | bytes 20608 | tf_op jit(solution)/shard_map/reduce_sum | solution.py:149
  146.4 3.1 %copy.27 = f32[64,8,2,1]{2,1,0,3:T(8,128)S(1)} copy(f32[64,8,2,1]{3,2,1,0:T(2,128)S(1)} %get-tuple-element.6) | data formatting | bytes 8192 | tf_op jit(solution)/shard_map/mul | solution.py:150
  149.5 0.7 fusion.36
  150.4 0.2 convolution_bitcast_fusion
  150.5 10.6 %all_to_all.21 = f32[8,4,256]{2,1,0:T(4,128)S(1)} all-to-all(f32[8,4,256]{2,1,0:T(4,128)S(1)} %bitcast.98), channel_id=1, replica_groups=mesh['y'=8,'z'=8,'core'=2,'heads'=4] {'heads','core'}, dimensions={0} | all-to-all | bytes 65536 | tf_op jit(solution)/shard_map/all_to_all | solution.py:157
  161.1 0.6 reduce_sum.82
  (35 shorter events, 1.5 us)
Async XLA Ops:
  6.5 41.2 %copy-start.1 = (bf16[5,64,1024]{2,1,0:T(8,128)(2,1)S(1)}, bf16[5,64,1024]{2,1,0:T(8,128)(2,1)}, u32[]{:S(2)}) copy-start(bf16[5,64,1024]{2,1,0:T(8,128)(2,1)} %param.9) | copy-start | bytes 1966084
  6.5 40.5 %copy-start = (bf16[512,1024]{1,0:T(8,128)(2,1)S(1)}, bf16[512,1024]{1,0:T(8,128)(2,1)}, u32[]{:S(2)}) copy-start(bf16[512,1024]{1,0:T(8,128)(2,1)} %param.12) | copy-start | bytes 3145732
  6.5 87.8 %all-gather.2.cloned.1.call-start = ((), (), s32[]{:S(2)}) async-start(), calls=%async_computation.4 | async-start | bytes 4718592 | tf_op jit(solution)/shard_map/all_gather | solution.py:98
  40.4 7.1 %collective-permute-start.1 = (bf16[5,16,1024]{2,1,0:T(8,128)(2,1)S(1)}, bf16[5,16,1024]{2,1,0:T(8,128)(2,1)S(1)}, u32[]{:S(2)}, u32[]{:S(2)}) collective-permute-start(bf16[5,16,1024]{2,1,0:T(8,128)(2,1)S(1)} %slice.57), channel_id=1, source_target_pairs={{8,0},{16,8},{24,16},{32,24},{40,32},{48,40},{56,48},{64,56},{72,6... | collective-permute-start | bytes 491528 | tf_op jit(solution)/shard_map/ppermute | solution.py:59
  41.0 6.6 %collective-permute-start.2 = (bf16[5,16,1024]{2,1,0:T(8,128)(2,1)S(1)}, bf16[5,16,1024]{2,1,0:T(8,128)(2,1)S(1)}, u32[]{:S(2)}, u32[]{:S(2)}) collective-permute-start(bf16[5,16,1024]{2,1,0:T(8,128)(2,1)S(1)} %slice.57), channel_id=1, source_target_pairs={{8,4},{16,12},{24,20},{32,28},{40,36},{48,44},{56,52},{64,60},{72,... | collective-permute-start | bytes 491528 | tf_op jit(solution)/shard_map/ppermute | solution.py:60
  42.3 5.4 %collective-permute-start = (bf16[5,64,1024]{2,1,0:T(8,128)(2,1)}, bf16[5,64,1024]{2,1,0:T(8,128)(2,1)S(1)}, u32[]{:S(2)}, u32[]{:S(2)}) collective-permute-start(bf16[5,64,1024]{2,1,0:T(8,128)(2,1)} %param.9), channel_id=1, source_target_pairs={{0,4},{4,0},{1,5},{5,1},{2,6},{6,2},{3,7},{7,3},{8,12},{12,8},{9,1... | collective-permute-start | bytes 1966088 | tf_op jit(solution)/shard_map/ppermute | solution.py:58
  101.3 11.2 %all-to-all-start.1 = ((bf16[8,128,128]{1,2,0:T(8,128)(2,1)}), bf16[8,128,128]{1,2,0:T(8,128)(2,1)S(1)}, u32[]{:S(2)}, u32[]{:S(2)}) async-start(bf16[8,128,128]{1,2,0:T(8,128)(2,1)} %broadcast_in_dim.5), calls=%async_computation.1 | async-start | bytes 524288 | tf_op jit(solution)/shard_map/all_to_all | solution.py:109
  117.9 24.8 %all-to-all-start.2 = ((bf16[64,16,128]{2,1,0:T(8,128)(2,1)}), bf16[64,16,128]{2,1,0:T(8,128)(2,1)S(1)}, u32[]{:S(2)}, u32[]{:S(2)}) async-start(bf16[64,16,128]{2,1,0:T(8,128)(2,1)} %pad_maximum_fusion.1), calls=%async_computation.2 | async-start | bytes 524288 | tf_op jit(solution)/shard_map/all_to_all | solution.py:142
Sparse Core Ops, SparseCore 0:
  39.5 53.6 all-gather.1
